TPU v7x, 256 devices: a whole 4x4x8 slice. The times are simulated.
256 devices in a mesh: rows: 64 (over z, x, core), cols: 4 (over y).
Axes of the slice: x: 4, y: 4, z: 8, core: 2. Of those that a mesh axis runs over, the one named last changes fastest.
Arguments:
- tiles: bfloat16 [64, 4, 32, 128, 128], P('rows', 'cols'), may hold values from -3 to 3
- tile_rows: int32 [64, 4, 32], P('rows', 'cols'), may hold values from 0 to 15
- tile_cols: int32 [64, 4, 32], P('rows', 'cols'), may hold values from 0 to 15
- tile_counts: int32 [64, 4], P('rows', 'cols'), may hold values from 16 to 32, as said below
- sketch: bfloat16 [4, 2048, 256], P('cols', 'rows'), may hold values from -6 to 6
Outputs:
- basis: float32 [131072, 256], P(('rows', 'cols'))
- factor: float32 [256, 256], replicated
Inputs may be any that keep to these rules, and one draw needn't show every extreme that they name: The live slots of a slab and column group are its first tile_counts slots; some slab and group has all 32 slots live.
All inputs are finite; a program needn't handle non-finite values.
Results may differ from a plain program's by a relative error of at most 0.004.
Values may be sent and summed in bfloat16 or wider, within the bound.
A program may use at most 64 MiB of HBM per device.

v0:
```python
import functools

import jax
import jax.numpy as jnp
from jax import lax
from jax.experimental import pallas as pl
from jax.experimental.pallas import tpu as pltpu
from jax.sharding import PartitionSpec as P

ROUNDS = 2
TR = 16
CGT = 16
TILE = 128
K = 256
SLOTS = 32
NZ = 8
NX = 4
NY = 4
PANEL = 64
W = 128
F32 = jnp.float32
BF16 = jnp.bfloat16
HI = lax.Precision.HIGHEST
MESH = pl.DeviceIdType.MESH
VM = pltpu.VMEM
MIB = 1024 * 1024


def order_kernel(rows_ref, cols_ref, count_ref, byrow_ref, bycol_ref, cnt_ref):
    live = count_ref[0]

    def one(key_ref, other_ref, out_ref):
        for b in range(TR + 1):
            cnt_ref[b] = 0

        def count(t, carry):
            b = jnp.where(t < live, key_ref[t], TR)
            cnt_ref[b] = cnt_ref[b] + 1
            return carry

        lax.fori_loop(0, SLOTS, count, 0)
        at = jnp.int32(0)
        for b in range(TR + 1):
            n = cnt_ref[b]
            cnt_ref[b] = at
            if b < TR:
                out_ref[112 + b] = jnp.where(n > 0, 1, 0)
                out_ref[96 + b] = jnp.maximum(at + n - 1, 0)
            at = at + n

        def clear(t, carry):
            out_ref[64 + t] = 1
            return carry

        lax.fori_loop(0, SLOTS, clear, 0)
        for b in range(TR + 1):
            first = cnt_ref[b]

            @pl.when(first < SLOTS)
            def _():
                out_ref[64 + first] = 0

        def place(t, carry):
            b = jnp.where(t < live, key_ref[t], TR)
            k = cnt_ref[b]
            cnt_ref[b] = k + 1
            out_ref[k] = t
            out_ref[32 + k] = other_ref[t]
            return carry

        lax.fori_loop(0, SLOTS, place, 0)

    one(rows_ref, cols_ref, byrow_ref)
    one(cols_ref, rows_ref, bycol_ref)


def slot_orders(rows_idx, cols_idx, count):
    smem = pl.BlockSpec(memory_space=pltpu.SMEM)
    out = jax.ShapeDtypeStruct((128,), jnp.int32)
    return pl.pallas_call(
        order_kernel,
        name="orders",
        out_shape=(out, out),
        in_specs=[smem] * 3,
        out_specs=[smem] * 2,
        scratch_shapes=[pltpu.SMEM((TR + 1,), jnp.int32)],
    )(rows_idx, cols_idx, count)


def spread(rows, q):
    return jnp.broadcast_to(rows[q : q + 1, :], (8, 128))


def factor_panel(lo, a_ref, e_ref, u_ref, x_ref):
    groups = PANEL // 8
    first = lo < 128
    a_half = (0, 1) if first else (1,)
    e_half = (0,) if first else (0, 1)
    n_a = len(a_half)
    sub = lax.broadcasted_iota(jnp.int32, (8, 128), 0)

    def rows_of(ref, g, halves):
        return [ref[lo + 8 * g : lo + 8 * g + 8, 128 * h : 128 * h + 128] for h in halves]

    rows = [rows_of(a_ref, g, a_half) + rows_of(e_ref, g, e_half) for g in range(groups)]
    for g in range(groups):
        c = (lo + 8 * g) % 128
        cols = [
            [jnp.broadcast_to(rows[i][0][:, c + q : c + q + 1], (8, 128)) for i in range(g, groups)]
            for q in range(8)
        ]
        done = []
        for q in range(8):
            inv = lax.rsqrt(spread(cols[q][0], q))
            cols[q] = [v * inv for v in cols[q]]
            for p in range(q + 1, 8):
                s = spread(cols[q][0], p)
                cols[p] = [v - w * s for v, w in zip(cols[p], cols[q])]
            row = [spread(v, q) for v in rows[g]]
            for w in range(q):
                s = spread(cols[w][0], q)
                row = [v - s * t for v, t in zip(row, done[w])]
            done.append([v * inv for v in row])
        out = done[0]
        for q in range(1, 8):
            out = [jnp.where(sub == q, v, o) for v, o in zip(done[q], out)]
        at = lo + 8 * g
        for h, v in zip(a_half, out[:n_a]):
            u_ref[at : at + 8, 128 * h : 128 * h + 128] = v
        for h, v in zip(e_half, out[n_a:]):
            x_ref[at : at + 8, 128 * h : 128 * h + 128] = v
        for i in range(g + 1, groups):
            for q in range(8):
                rows[i] = [v - cols[q][i - g] * t for v, t in zip(rows[i], done[q])]
    hi = lo + PANEL
    if hi < K:
        dn = (((0,), (0,)), ((), ()))
        a0 = 0 if hi < 128 else 128
        width = 128 if first else K
        u = u_ref[lo:hi, a0:]
        a_ref[a0:, a0:] -= lax.dot_general(u, u, dn, precision=HI, preferred_element_type=F32)
        e_ref[a0:, :width] -= lax.dot_general(
            u, x_ref[lo:hi, :width], dn, precision=HI, preferred_element_type=F32
        )


def factor_start(gram, a_ref, e_ref, u_ref, x_ref):
    a_ref[...] = gram
    row_i = lax.broadcasted_iota(jnp.int32, (K, K), 0)
    col_i = lax.broadcasted_iota(jnp.int32, (K, K), 1)
    e_ref[...] = jnp.where(row_i == col_i, 1.0, 0.0)
    x_ref[:128, 128:] = jnp.zeros((128, 128), F32)
    u_ref[128:, :128] = jnp.zeros((128, 128), F32)


def factor_kernel(scale, g_ref, y_ref, q_ref, u_ref, x_ref, a_ref, e_ref):
    factor_start(g_ref[...] * scale, a_ref, e_ref, u_ref, x_ref)
    for lo in range(0, K, PANEL):
        factor_panel(lo, a_ref, e_ref, u_ref, x_ref)
    row_i = lax.broadcasted_iota(jnp.int32, (K, K), 0)
    col_i = lax.broadcasted_iota(jnp.int32, (K, K), 1)
    u_ref[...] = jnp.where(col_i >= row_i, u_ref[...], 0.0)
    q_ref[...] = apply_inverse(y_ref[...], x_ref[...])


def apply_inverse(share, inverse):
    return lax.dot_general(
        share, inverse, (((1,), (1,)), ((), ())), precision=HI, preferred_element_type=F32
    )


def factorize(gram, scale, share):
    vmem = pl.BlockSpec(memory_space=VM)
    square = jax.ShapeDtypeStruct((K, K), F32)
    return pl.pallas_call(
        functools.partial(factor_kernel, scale),
        name="factor_apply",
        out_shape=(jax.ShapeDtypeStruct(share.shape, F32), square),
        in_specs=[vmem] * 2,
        out_specs=[vmem] * 2,
        scratch_shapes=[pltpu.VMEM((K, K), F32)] * 3,
        compiler_params=pltpu.CompilerParams(vmem_limit_bytes=32 * MIB),
    )(gram, share)


class Net:
    def __init__(self, send, recv, base):
        self.send, self.recv, self.base, self.copies = send, recv, base, []

    def start(self, src, dst, device):
        k = self.base + len(self.copies)
        copy = pltpu.make_async_remote_copy(
            src_ref=src,
            dst_ref=dst,
            send_sem=self.send.at[k],
            recv_sem=self.recv.at[k],
            device_id=device,
            device_id_type=MESH,
        )
        copy.start()
        self.copies.append(copy)
        return copy

    def drain(self):
        for copy in self.copies:
            copy.wait_send()


def ring4(me):
    return lax.rem(me + 1, 4), lax.rem(me + 3, 4), lax.rem(me + 2, 4)


def gather4(net, loc, me, to, arrived=None):
    arrived = arrived or (lambda p: None)
    right, left, opp = ring4(me)
    r_a = net.start(loc(me, 0), loc(me, 0), to(right))
    l_b = net.start(loc(me, 1), loc(me, 1), to(left))
    r_b = net.start(loc(me, 1), loc(me, 1), to(right))
    l_a = net.start(loc(me, 0), loc(me, 0), to(left))
    arrived(me)
    yield
    r_a.wait_recv()
    f_a = net.start(loc(left, 0), loc(left, 0), to(right))
    l_b.wait_recv()
    f_b = net.start(loc(right, 1), loc(right, 1), to(left))
    yield
    r_b.wait_recv()
    arrived(left)
    l_a.wait_recv()
    arrived(right)
    f_a.wait_recv()
    f_b.wait_recv()
    arrived(opp)


def gather_rows(net, x_ref, where, to_z, to_x, other_core):
    z, x, core = where
    spot = x_ref.at[z, lax.div(x, 2), lax.rem(x, 2), core]
    copies = [net.start(spot, spot, to_z(lax.rem(z + d, NZ))) for d in range(1, NZ)]
    yield
    for copy in copies:
        copy.wait_recv()
    crossing = []

    def cross(p):
        spot = x_ref.at[:, lax.div(p, 2), lax.rem(p, 2), core]
        crossing.append(net.start(spot, spot, other_core))

    def loc(p, h):
        return x_ref.at[pl.ds(h * (NZ // 2), NZ // 2), lax.div(p, 2), lax.rem(p, 2), core]

    yield from gather4(net, loc, x, to_x, cross)
    for copy in crossing:
        copy.wait_recv()


def scatter4(net, src, me, to, buf, tmp, store, ready=None):
    right, left, opp = ring4(me)
    ready = ready or (lambda p: None)
    ready(opp)
    a0 = net.start(src(opp, 0), buf.at[0], to(right))
    b0 = net.start(src(opp, 1), buf.at[1], to(left))
    ready(right)
    b1 = net.start(src(right, 1), buf.at[2], to(right))
    ready(left)
    a1 = net.start(src(left, 0), buf.at[3], to(left))
    yield
    a0.wait_recv()
    tmp[0] = src(right, 0)[...] + buf[0]
    a2 = net.start(tmp.at[0], buf.at[4], to(right))
    b0.wait_recv()
    tmp[1] = src(left, 1)[...] + buf[1]
    b2 = net.start(tmp.at[1], buf.at[5], to(left))
    ready(me)
    yield
    a1.wait_recv()
    b1.wait_recv()
    a2.wait_recv()
    store(0, src(me, 0)[...] + (buf[3] + buf[4]))
    b2.wait_recv()
    store(1, src(me, 1)[...] + (buf[2] + buf[5]))


def scatter_rows(net, part_ref, refs, where, to_z, to_x, other_core, out):
    z, x, core = where
    buf_ref, tmp_ref, r0_ref, c1_ref, c2_ref, rz_ref = refs
    right, left, opp = ring4(x)
    crossing = []
    for p in (opp, right, left, x):
        src = part_ref.at[:, lax.div(p, 2), lax.rem(p, 2), 1 - core]
        crossing.append(net.start(src, r0_ref.at[p], other_core))
    arriving = iter(crossing)
    yield

    def ready(p):
        next(arriving).wait_recv()
        c1_ref[p] = part_ref[:, lax.div(p, 2), lax.rem(p, 2), core] + r0_ref[p]

    def store(h, value):
        c2_ref[pl.ds(h * (NZ // 2), NZ // 2)] = value

    def src(p, h):
        return c1_ref.at[p, pl.ds(h * (NZ // 2), NZ // 2)]

    yield from scatter4(net, src, x, to_x, buf_ref, tmp_ref, store, ready)
    copies = []
    for d in range(1, NZ):
        p = lax.rem(z + d, NZ)
        copies.append(net.start(c2_ref.at[p], rz_ref.at[d - 1], to_z(p)))
    yield
    total = c2_ref[z]
    for d, copy in enumerate(copies):
        copy.wait_recv()
        total = total + rz_ref[d]
    out.append(total)


def gram_sum(net, share, refs, where, to_z, to_q, to_y):
    g_ref, g1_ref, s1_ref, g2_ref, s2_ref, g3_ref, gf_ref = refs
    z, x, core, q, y = where
    gram = lax.dot_general(
        share, share, (((0,), (0,)), ((), ())), precision=HI, preferred_element_type=F32
    )
    g_ref[0] = gram[:, :128]
    g_ref[1] = gram[:, 128:]
    wide, thin = K // NX, K // NX // NZ
    copies = []
    for d in range(1, 2 * NX):
        p = lax.rem(q + d, 2 * NX)
        src = g_ref.at[lax.rem(p, 2), pl.ds(pl.multiple_of(lax.div(p, 2) * wide, wide), wide)]
        copies.append(net.start(src, g1_ref.at[d - 1], to_q(p)))
    yield
    total = g_ref[core, pl.ds(pl.multiple_of(x * wide, wide), wide)]
    for d, copy in enumerate(copies):
        copy.wait_recv()
        total = total + g1_ref[d]
    s1_ref[...] = total
    copies = []
    for d in range(1, NZ):
        p = lax.rem(z + d, NZ)
        src = s1_ref.at[pl.ds(pl.multiple_of(p * thin, thin), thin)]
        copies.append(net.start(src, g2_ref.at[d - 1], to_z(p)))
    yield
    total = s1_ref[pl.ds(pl.multiple_of(z * thin, thin), thin)]
    for d, copy in enumerate(copies):
        copy.wait_recv()
        total = total + g2_ref[d]
    g3_ref[y] = total
    spot = g3_ref.at[y]
    copies = [net.start(spot, spot, to_y(lax.rem(y + d, NY))) for d in range(1, NY)]
    yield
    for copy in copies:
        copy.wait_recv()
    total = (g3_ref[0] + g3_ref[1]) + (g3_ref[2] + g3_ref[3])
    at_thin = pl.ds(pl.multiple_of(x * wide + z * thin, thin), thin)
    gf_ref[core, at_thin] = total
    spot = gf_ref.at[core, at_thin]
    copies = [net.start(spot, spot, to_z(lax.rem(z + d, NZ))) for d in range(1, NZ)]
    yield
    for copy in copies:
        copy.wait_recv()
    spot = gf_ref.at[core, pl.ds(pl.multiple_of(x * wide, wide), wide)]
    copies = [net.start(spot, spot, to_q(lax.rem(q + d, 2 * NX))) for d in range(1, 2 * NX)]
    yield
    for copy in copies:
        copy.wait_recv()


def tile_products(tiles_ref, order_ref, load, prefix_ref, store, transposed, twice):
    dn = (((0,), (0,)), ((), ())) if transposed else (((1,), (0,)), ((), ()))

    def step(k, acc):
        tile = tiles_ref[order_ref[k]]
        if twice:
            tile = jnp.concatenate([tile, tile], axis=0 if transposed else 1)
        prod = lax.dot_general(tile, load(order_ref[32 + k]), dn, preferred_element_type=F32)
        acc = acc * order_ref[64 + k].astype(F32) + prod
        prefix_ref[k] = acc
        return acc

    lax.fori_loop(0, SLOTS, step, jnp.zeros((TILE, W), F32), unroll=8)
    for b in range(TR):
        store(b, prefix_ref[order_ref[96 + b]] * order_ref[112 + b].astype(F32))


def two_parts(value):
    high = value.astype(BF16)
    return high, (value - high.astype(F32)).astype(BF16)


def step(*running):
    for stage in running:
        next(stage, None)


def scratch_shapes():
    wide, thin = K // NX, K // NX // NZ
    shapes = {
        "x_first0": ((NZ, 2, 2, 2, 1, 32, W), BF16),
        "x_first1": ((NZ, 2, 2, 2, 1, 32, W), BF16),
        "x_rows0": ((NZ, 2, 2, 2, 2, 32, W), BF16),
        "x_rows1": ((NZ, 2, 2, 2, 2, 32, W), BF16),
        "x_columns0": ((NY, 2, 2, 2, TILE, W), BF16),
        "x_columns1": ((NY, 2, 2, 2, TILE, W), BF16),
        "prefix": ((SLOTS, TILE, W), F32),
        "part_rows": ((2, NY, 2, 2, TILE, W), F32),
        "part_columns": ((2, NZ, 2, 2, 2, 32, W), F32),
        "buf_rows": ((2, 6, 2, TILE, W), F32),
        "tmp_rows": ((2, 2, 2, TILE, W), F32),
        "buf_columns": ((2, 6, NZ // 2, 32, W), F32),
        "tmp_columns": ((2, 2, NZ // 2, 32, W), F32),
        "r0": ((2, NX, NZ, 32, W), F32),
        "c1": ((2, NX, NZ, 32, W), F32),
        "c2": ((2, NZ, 32, W), F32),
        "rz": ((2, NZ - 1, 32, W), F32),
        "g": ((2, 2, K, 128), F32),
        "g1": ((2, 2 * NX - 1, wide, 128), F32),
        "s1": ((2, wide, 128), F32),
        "g2": ((2, NZ - 1, thin, 128), F32),
        "s2": ((2, thin, 128), F32),
        "g3": ((2, NY, thin, 128), F32),
        "gf": ((2, 2, K, 128), F32),
        "a": ((K, K), F32),
        "e": ((K, K), F32),
        "u": ((K, K), F32),
        "inverse": ((K, K), F32),
        "y_share": ((4 * TILE, K), F32),
        "z_share": ((32, K), F32),
    }
    return {name: VM(shape, dtype) for name, (shape, dtype) in shapes.items()}


FIRST, COLUMNS, ROWS, LAST = 0, 60, 150, 240
COPIES = 280


def power_kernel(
    row_scale, column_scale, sketch_ref, tiles_ref, byrow_ref, bycol_ref, share_ref, gram_ref, *refs
):
    send, recv = refs[:2]
    ref = dict(zip(scratch_shapes(), refs[2:]))
    row, y = lax.axis_index("rows"), lax.axis_index("cols")
    core = lax.rem(row, 2)
    x = lax.rem(lax.div(row, 2), NX)
    z = lax.div(row, 2 * NX)
    q = lax.rem(row, 2 * NX)

    def at(z_, q_, y_):
        return (z_ * (2 * NX) + q_, y_)

    to_z = lambda p: at(p, q, y)
    to_q = lambda p: at(z, p, y)
    to_x = lambda p: at(z, p * 2 + core, y)
    to_y = lambda p: at(z, q, p)
    other_core = at(z, x * 2 + (1 - core), y)

    barrier = pltpu.get_barrier_semaphore()
    for d in range(1, NZ):
        pl.semaphore_signal(barrier, 1, device_id=to_z(lax.rem(z + d, NZ)), device_id_type=MESH)
    for d in range(1, 2 * NX):
        pl.semaphore_signal(barrier, 1, device_id=to_q(lax.rem(q + d, 2 * NX)), device_id_type=MESH)
    for d in range(1, NY):
        pl.semaphore_signal(barrier, 1, device_id=to_y(lax.rem(y + d, NY)), device_id_type=MESH)
    pl.semaphore_wait(barrier, NZ - 1 + 2 * NX - 1 + NY - 1)

    def gram_of(net, share, parity):
        refs = [ref[name].at[parity] for name in ("g", "g1", "s1", "g2", "s2", "g3", "gf")]
        return gram_sum(net, share, refs, (z, x, core, q, y), to_z, to_q, to_y)

    def half_columns(net, h, value, out):
        xs, part = ref["x_columns" + str(h)], ref["part_columns"].at[h]
        for i, v in enumerate(value):
            xs[y, :, :, i] = v.reshape(2, 2, TILE, W)
        gather = gather4(net, lambda p, i: xs.at[p, i], y, to_y)
        names = ("buf_columns", "tmp_columns", "r0", "c1", "c2", "rz")
        buffers = [ref[name].at[h] for name in names]
        scatter = scatter_rows(net, part, buffers, (z, x, core), to_z, to_x, other_core, out)

        def load(b):
            return xs[b >> 2, (b >> 1) & 1, b & 1].reshape(2 * TILE, W)

        def keep(b, value):
            part[b // 2, b % 2] = value.reshape(2, 2, 32, W)

        def products():
            tile_products(tiles_ref, bycol_ref, load, ref["prefix"], keep, True, True)

        return gather, products, scatter

    def half_rows(net, h, value, out):
        xs = ref[("x_first" if len(value) == 1 else "x_rows") + str(h)]
        part = ref["part_rows"].at[h]
        for i, v in enumerate(value):
            xs[z, lax.div(x, 2), lax.rem(x, 2), core, i] = v
        gather = gather_rows(net, xs, (z, x, core), to_z, to_x, other_core)

        def store(i, value):
            out.append(value.reshape(2 * TILE, W))

        scatter = scatter4(
            net,
            lambda p, i: part.at[p, i],
            y,
            to_y,
            ref["buf_rows"].at[h],
            ref["tmp_rows"].at[h],
            store,
        )

        def load(b):
            both = xs[b >> 1, b & 1]
            parts = [both[:, :, i].reshape(TILE, W) for i in range(both.shape[2])]
            return parts[0] if len(parts) == 1 else jnp.concatenate(parts, axis=0)

        def keep(b, value):
            part[b // 4, (b // 2) % 2, b % 2] = value

        def products():
            tile_products(tiles_ref, byrow_ref, load, ref["prefix"], keep, False, len(value) == 2)

        return gather, products, scatter

    def panel(i):
        factor_panel(i * PANEL, ref["a"], ref["e"], ref["u"], ref["inverse"])

    def factor_begin(scale, parity):
        full = jnp.concatenate([ref["gf"][parity, 0], ref["gf"][parity, 1]], axis=1)
        factor_start(full * scale, ref["a"], ref["e"], ref["u"], ref["inverse"])

    def put(out, share):
        for i, halves in enumerate(zip(*out)):
            value = apply_inverse(jnp.concatenate(halves, axis=1), ref["inverse"][...])
            share[i * value.shape[0] : (i + 1) * value.shape[0], :] = value

    def first():
        net, out = Net(send, recv, FIRST), ([], [])
        g0, p0, s0 = half_rows(net, 0, (sketch_ref[:, :W],), out[0])
        g1, p1, s1 = half_rows(net, 1, (sketch_ref[:, W:],), out[1])
        step(g0, g0, g1, g0, g0)
        p0()
        step(s0, g1, g1, s0, g1)
        p1()
        step(s1, s0, s1, s1)
        for h in range(2):
            for i in range(2):
                ref["y_share"][i * 2 * TILE : (i + 1) * 2 * TILE, h * W : (h + 1) * W] = out[h][i]
        net.drain()

    def columns():
        net, out = Net(send, recv, COLUMNS), ([], [])
        share = ref["y_share"]
        gram = gram_of(net, share[...], 0)
        g0, p0, s0 = half_columns(net, 0, two_parts(share[:, :W]), out[0])
        g1, p1, s1 = half_columns(net, 1, two_parts(share[:, W:]), out[1])
        step(g0, gram, gram, g0, g1, gram, g0)
        p0()
        step(s0, g1, gram, s0, g1)
        p1()
        step(s1, gram, s0, s1, gram)
        factor_begin(row_scale, 0)
        panel(0)
        step(s0, s1)
        panel(1)
        step(s1)
        panel(2)
        panel(3)
        step(s0, s1)
        put(out, ref["z_share"])
        net.drain()

    def rows():
        net, out = Net(send, recv, ROWS), ([], [])
        share = ref["z_share"]
        gram = gram_of(net, share[...], 1)
        g0, p0, s0 = half_rows(net, 0, two_parts(share[:, :W]), out[0])
        g1, p1, s1 = half_rows(net, 1, two_parts(share[:, W:]), out[1])
        step(g0, gram, g0, g1, gram, g0, gram, g0)
        p0()
        step(s0, g1, gram, g1, s0, gram, g1)
        p1()
        step(s1, gram)
        factor_begin(column_scale, 1)
        panel(0)
        panel(1)
        step(s0, s1)
        panel(2)
        panel(3)
        step(s1)
        put(out, ref["y_share"])
        net.drain()

    def one_round(i, carry):
        columns()
        rows()
        return carry

    first()
    lax.fori_loop(0, ROUNDS, one_round, 0)
    net = Net(send, recv, LAST)
    for stage in gram_of(net, ref["y_share"][...], 0):
        pass
    share_ref[...] = ref["y_share"][...]
    gram_ref[:, :128] = ref["gf"][0, 0]
    gram_ref[:, 128:] = ref["gf"][0, 1]
    net.drain()


def power(sketch, tiles, by_row, by_col, row_scale, column_scale):
    vmem, smem = pl.BlockSpec(memory_space=VM), pl.BlockSpec(memory_space=pltpu.SMEM)
    return pl.pallas_call(
        functools.partial(power_kernel, row_scale, column_scale),
        name="power",
        out_shape=(
            jax.ShapeDtypeStruct((4 * TILE, K), F32),
            jax.ShapeDtypeStruct((K, K), F32),
        ),
        in_specs=[vmem, vmem, smem, smem],
        out_specs=[vmem, vmem],
        scratch_shapes=[pltpu.SemaphoreType.DMA((COPIES,))] * 2 + list(scratch_shapes().values()),
        compiler_params=pltpu.CompilerParams(
            collective_id=1, has_side_effects=True, vmem_limit_bytes=48 * MIB
        ),
    )(sketch, tiles, by_row, by_col)


def shards(tiles, tile_rows, tile_cols, tile_counts, sketch):
    row_scale = 1.0 / (TR * TILE * lax.axis_size("rows"))
    column_scale = 1.0 / (CGT * TILE * lax.axis_size("cols"))
    by_row, by_col = slot_orders(tile_rows[0, 0], tile_cols[0, 0], tile_counts[0])
    share, gram = power(sketch[0], tiles[0, 0], by_row, by_col, row_scale, column_scale)
    return factorize(gram, row_scale, share)


def solution(mesh):
    return jax.shard_map(
        shards,
        mesh=mesh,
        in_specs=(
            P("rows", "cols", None, None, None),
            P("rows", "cols", None),
            P("rows", "cols", None),
            P("rows", "cols"),
            P("cols", "rows", None),
        ),
        out_specs=(P(("rows", "cols"), None), P()),
        check_vma=False,
    )
```

profile of v0, /device:TPU:1, one launch (start us, length us, event | category | flops | bytes accessed | tf_op | source)
XLA Modules:
  0.0 246.3 jit_solution(6079341743423790057)
XLA Ops:
  0.6 0.0 copy-start.1
  1.3 3.1 %orders.1 = (s32[128]{0:T(128)}, s32[128]{0:T(128)}) custom-call(s32[32]{0:T(128)} %bitcast.8, s32[32]{0:T(128)} %bitcast.9, s32[1]{0:T(128)} %bitcast.5.count_ref), custom_call_target="tpu_custom_call" | custom-call | tf_op jit(solution)/shard_map/orders/pallas_call | solution.py:80
  4.4 0.0 copy-start.2
  4.4 0.0 copy-start.3
  4.4 0.0 copy-done.1
  4.4 0.6 copy-done.2
  5.0 0.0 copy-done.3
  5.0 0.0 copy-start
  5.0 1.2 copy-done
  6.3 230.6 %power.1 = (f32[512,256]{1,0:T(8,128)S(1)}, f32[256,256]{1,0:T(8,128)S(1)}) custom-call(bf16[32,256]{1,0:T(8,128)(2,1)S(1)} %bitcast.7, bf16[32,128,128]{2,1,0:T(8,128)(2,1)S(1)} %bitcast.6, s32[128]{0:T(128)S(1)} %copy-done.2, s32[128]{0:T(128)S(1)} %copy-done.3), custom_call_target="tpu_custom_call" | custom-call | tf_op jit(solution)/shard_map/power/pallas_call | solution.py:610
  236.8 9.4 %factor_apply.1 = (f32[512,256]{1,0:T(8,128)}, f32[256,256]{1,0:T(8,128)}) custom-call(f32[256,256]{1,0:T(8,128)S(1)} %get-tuple-element.8.g_ref, f32[512,256]{1,0:T(8,128)S(1)} %get-tuple-element.9.y_ref), custom_call_target="tpu_custom_call" | custom-call | tf_op jit(solution)/shard_map/factor_apply/pallas_call | solution.py:175
Async XLA Ops:
  0.6 3.8 %copy-start.1 = (bf16[1,32,256]{2,1,0:T(8,128)(2,1)S(1)}, bf16[1,32,256]{2,1,0:T(8,128)(2,1)}, u32[]{:S(2)}) copy-start(bf16[1,32,256]{2,1,0:T(8,128)(2,1)} %param.9) | copy-start | bytes 49156
  4.4 0.7 copy-start.2
  4.4 0.6 copy-start.3
  5.0 1.2 copy-start
where the time goes:
time: 246 us
  Pallas kernels  243 us (99%)
    pallas_call x1, Pallas kernels, power(): pl.pallas_call(functools.partial(power_kernel, row_scale, column_scale),...  231 us
    pallas_call x1, Pallas kernels, factorize(): pl.pallas_call(functools.partial(factor_kernel, scale), name='factor_appl...  9.44 us

commit v1 on v0

--- a/solution.py
+++ b/solution.py
@@ -18,6 +18,7 @@
 NY = 4
 PANEL = 64
 W = 128
+THIN = K // (NX * NY)
 F32 = jnp.float32
 BF16 = jnp.bfloat16
 HI = lax.Precision.HIGHEST
@@ -38,7 +39,7 @@
             cnt_ref[b] = cnt_ref[b] + 1
             return carry
 
-        lax.fori_loop(0, SLOTS, count, 0)
+        lax.fori_loop(0, SLOTS, count, 0, unroll=True)
         at = jnp.int32(0)
         for b in range(TR + 1):
             n = cnt_ref[b]
@@ -52,7 +53,7 @@
             out_ref[64 + t] = 1
             return carry
 
-        lax.fori_loop(0, SLOTS, clear, 0)
+        lax.fori_loop(0, SLOTS, clear, 0, unroll=True)
         for b in range(TR + 1):
             first = cnt_ref[b]
 
@@ -68,7 +69,7 @@
             out_ref[32 + k] = other_ref[t]
             return carry
 
-        lax.fori_loop(0, SLOTS, place, 0)
+        lax.fori_loop(0, SLOTS, place, 0, unroll=True)
 
     one(rows_ref, cols_ref, byrow_ref)
     one(cols_ref, rows_ref, bycol_ref)
@@ -315,55 +316,48 @@
     out.append(total)
 
 
-def gram_sum(net, share, refs, where, to_z, to_q, to_y):
-    g_ref, g1_ref, s1_ref, g2_ref, s2_ref, g3_ref, gf_ref = refs
-    z, x, core, q, y = where
+def gram_sum(net, share, refs, where, to_z, to_xy, other_core):
+    g_ref, g0_ref, s0_ref, g1_ref, g2_ref, gf_ref = refs
+    z, w, core = where
     gram = lax.dot_general(
         share, share, (((0,), (0,)), ((), ())), precision=HI, preferred_element_type=F32
     )
     g_ref[0] = gram[:, :128]
     g_ref[1] = gram[:, 128:]
-    wide, thin = K // NX, K // NX // NZ
-    copies = []
-    for d in range(1, 2 * NX):
-        p = lax.rem(q + d, 2 * NX)
-        src = g_ref.at[lax.rem(p, 2), pl.ds(pl.multiple_of(lax.div(p, 2) * wide, wide), wide)]
-        copies.append(net.start(src, g1_ref.at[d - 1], to_q(p)))
-    yield
-    total = g_ref[core, pl.ds(pl.multiple_of(x * wide, wide), wide)]
+    crossing = net.start(g_ref.at[1 - core], g0_ref, other_core)
+    yield
+    crossing.wait_recv()
+    s0_ref[...] = g_ref[core] + g0_ref[...]
+
+    def piece(p):
+        return pl.ds(pl.multiple_of(p * THIN, THIN), THIN)
+
+    others = [lax.rem(w + d, NX * NY) for d in range(1, NX * NY)]
+    copies = [net.start(s0_ref.at[piece(p)], g1_ref.at[d], to_xy(p)) for d, p in enumerate(others)]
+    yield
+    total = s0_ref[piece(w)]
     for d, copy in enumerate(copies):
         copy.wait_recv()
         total = total + g1_ref[d]
-    s1_ref[...] = total
-    copies = []
-    for d in range(1, NZ):
-        p = lax.rem(z + d, NZ)
-        src = s1_ref.at[pl.ds(pl.multiple_of(p * thin, thin), thin)]
-        copies.append(net.start(src, g2_ref.at[d - 1], to_z(p)))
-    yield
-    total = s1_ref[pl.ds(pl.multiple_of(z * thin, thin), thin)]
-    for d, copy in enumerate(copies):
-        copy.wait_recv()
-        total = total + g2_ref[d]
-    g3_ref[y] = total
-    spot = g3_ref.at[y]
-    copies = [net.start(spot, spot, to_y(lax.rem(y + d, NY))) for d in range(1, NY)]
+    g2_ref[z] = total
+    spot = g2_ref.at[z]
+    copies = [net.start(spot, spot, to_z(lax.rem(z + d, NZ))) for d in range(1, NZ)]
     yield
     for copy in copies:
         copy.wait_recv()
-    total = (g3_ref[0] + g3_ref[1]) + (g3_ref[2] + g3_ref[3])
-    at_thin = pl.ds(pl.multiple_of(x * wide + z * thin, thin), thin)
-    gf_ref[core, at_thin] = total
-    spot = gf_ref.at[core, at_thin]
-    copies = [net.start(spot, spot, to_z(lax.rem(z + d, NZ))) for d in range(1, NZ)]
+    total = g2_ref[0]
+    for d in range(1, NZ):
+        total = total + g2_ref[d]
+    gf_ref[core, piece(w)] = total
+    spot = gf_ref.at[core, piece(w)]
+    copies = [net.start(spot, spot, to_xy(p)) for p in others]
     yield
     for copy in copies:
         copy.wait_recv()
-    spot = gf_ref.at[core, pl.ds(pl.multiple_of(x * wide, wide), wide)]
-    copies = [net.start(spot, spot, to_q(lax.rem(q + d, 2 * NX))) for d in range(1, 2 * NX)]
-    yield
-    for copy in copies:
-        copy.wait_recv()
+    spot = gf_ref.at[core]
+    crossing = net.start(spot, spot, other_core)
+    yield
+    crossing.wait_recv()
 
 
 def tile_products(tiles_ref, order_ref, load, prefix_ref, store, transposed, twice):
@@ -394,7 +388,6 @@
 
 
 def scratch_shapes():
-    wide, thin = K // NX, K // NX // NZ
     shapes = {
         "x_first0": ((NZ, 2, 2, 2, 1, 32, W), BF16),
         "x_first1": ((NZ, 2, 2, 2, 1, 32, W), BF16),
@@ -414,11 +407,10 @@
         "c2": ((2, NZ, 32, W), F32),
         "rz": ((2, NZ - 1, 32, W), F32),
         "g": ((2, 2, K, 128), F32),
-        "g1": ((2, 2 * NX - 1, wide, 128), F32),
-        "s1": ((2, wide, 128), F32),
-        "g2": ((2, NZ - 1, thin, 128), F32),
-        "s2": ((2, thin, 128), F32),
-        "g3": ((2, NY, thin, 128), F32),
+        "g0": ((2, K, 128), F32),
+        "s0": ((2, K, 128), F32),
+        "g1": ((2, NX * NY - 1, THIN, 128), F32),
+        "g2": ((2, NZ, THIN, 128), F32),
         "gf": ((2, 2, K, 128), F32),
         "a": ((K, K), F32),
         "e": ((K, K), F32),
@@ -430,8 +422,8 @@
     return {name: VM(shape, dtype) for name, (shape, dtype) in shapes.items()}
 
 
-FIRST, COLUMNS, ROWS, LAST = 0, 60, 150, 240
-COPIES = 280
+FIRST, COLUMNS, ROWS, LAST = 0, 60, 160, 260
+COPIES = 310
 
 
 def power_kernel(
@@ -444,12 +436,13 @@
     x = lax.rem(lax.div(row, 2), NX)
     z = lax.div(row, 2 * NX)
     q = lax.rem(row, 2 * NX)
+    w = x * NY + y
 
     def at(z_, q_, y_):
         return (z_ * (2 * NX) + q_, y_)
 
     to_z = lambda p: at(p, q, y)
-    to_q = lambda p: at(z, p, y)
+    to_xy = lambda p: at(z, lax.div(p, NY) * 2 + core, lax.rem(p, NY))
     to_x = lambda p: at(z, p * 2 + core, y)
     to_y = lambda p: at(z, q, p)
     other_core = at(z, x * 2 + (1 - core), y)
@@ -457,15 +450,15 @@
     barrier = pltpu.get_barrier_semaphore()
     for d in range(1, NZ):
         pl.semaphore_signal(barrier, 1, device_id=to_z(lax.rem(z + d, NZ)), device_id_type=MESH)
-    for d in range(1, 2 * NX):
-        pl.semaphore_signal(barrier, 1, device_id=to_q(lax.rem(q + d, 2 * NX)), device_id_type=MESH)
-    for d in range(1, NY):
-        pl.semaphore_signal(barrier, 1, device_id=to_y(lax.rem(y + d, NY)), device_id_type=MESH)
-    pl.semaphore_wait(barrier, NZ - 1 + 2 * NX - 1 + NY - 1)
+    for d in range(1, NX * NY):
+        other = to_xy(lax.rem(w + d, NX * NY))
+        pl.semaphore_signal(barrier, 1, device_id=other, device_id_type=MESH)
+    pl.semaphore_signal(barrier, 1, device_id=other_core, device_id_type=MESH)
+    pl.semaphore_wait(barrier, NZ - 1 + NX * NY - 1 + 1)
 
     def gram_of(net, share, parity):
-        refs = [ref[name].at[parity] for name in ("g", "g1", "s1", "g2", "s2", "g3", "gf")]
-        return gram_sum(net, share, refs, (z, x, core, q, y), to_z, to_q, to_y)
+        refs = [ref[name].at[parity] for name in ("g", "g0", "s0", "g1", "g2", "gf")]
+        return gram_sum(net, share, refs, (z, w, core), to_z, to_xy, other_core)
 
     def half_columns(net, h, value, out):
         xs, part = ref["x_columns" + str(h)], ref["part_columns"].at[h]

time: 246 us -> 241 us (0.980)
  Pallas kernels: 243 us -> 237 us
    pallas_call x1, Pallas kernels: 231 us -> 226 us  [power(): pl.pallas_call(functools.partial(power_kernel, row_scale, column_scale),...]
where the time goes in v1:
time: 241 us
  Pallas kernels  237 us (98%)
    pallas_call x1, Pallas kernels, power(): pl.pallas_call(functools.partial(power_kernel, row_scale, column_scale),...  226 us
    pallas_call x1, Pallas kernels, factorize(): pl.pallas_call(functools.partial(factor_kernel, scale), name='factor_appl...  9.44 us

profile of v1, /device:TPU:1, one launch (start us, length us, event | category | flops | bytes accessed | tf_op | source)
XLA Modules:
  0.0 240.6 jit_solution(14138746203970528498)
XLA Ops:
  0.6 0.0 copy-start.1
  1.3 1.9 orders.1
  3.2 0.0 copy-start.2
  3.2 0.0 copy-start.3
  3.2 0.0 copy-done.1
  3.3 0.6 copy-done.2
  3.9 0.0 copy-done.3
  3.9 0.0 copy-start
  3.9 1.2 copy-done
  5.1 226.0 %power.1 = (f32[512,256]{1,0:T(8,128)S(1)}, f32[256,256]{1,0:T(8,128)S(1)}) custom-call(bf16[32,256]{1,0:T(8,128)(2,1)S(1)} %bitcast.7, bf16[32,128,128]{2,1,0:T(8,128)(2,1)S(1)} %bitcast.6, s32[128]{0:T(128)S(1)} %copy-done.2, s32[128]{0:T(128)S(1)} %copy-done.3), custom_call_target="tpu_custom_call" | custom-call | tf_op jit(solution)/shard_map/power/pallas_call | solution.py:603
  231.2 9.4 %factor_apply.1 = (f32[512,256]{1,0:T(8,128)}, f32[256,256]{1,0:T(8,128)}) custom-call(f32[256,256]{1,0:T(8,128)S(1)} %get-tuple-element.8.g_ref, f32[512,256]{1,0:T(8,128)S(1)} %get-tuple-element.9.y_ref), custom_call_target="tpu_custom_call" | custom-call | tf_op jit(solution)/shard_map/factor_apply/pallas_call | solution.py:176
Async XLA Ops:
  0.6 2.6 %copy-start.1 = (bf16[1,32,256]{2,1,0:T(8,128)(2,1)S(1)}, bf16[1,32,256]{2,1,0:T(8,128)(2,1)}, u32[]{:S(2)}) copy-start(bf16[1,32,256]{2,1,0:T(8,128)(2,1)} %param.9) | copy-start | bytes 49156
  3.2 0.7 copy-start.2
  3.2 0.6 copy-start.3
  3.9 1.2 copy-start

commit v2 on v1

--- a/solution.py
+++ b/solution.py
@@ -395,6 +395,7 @@
         "x_rows1": ((NZ, 2, 2, 2, 2, 32, W), BF16),
         "x_columns0": ((NY, 2, 2, 2, TILE, W), BF16),
         "x_columns1": ((NY, 2, 2, 2, TILE, W), BF16),
+        "tiles": ((SLOTS, TILE, TILE), BF16),
         "prefix": ((SLOTS, TILE, W), F32),
         "part_rows": ((2, NY, 2, 2, TILE, W), F32),
         "part_columns": ((2, NZ, 2, 2, 2, 32, W), F32),
@@ -427,10 +428,13 @@
 
 
 def power_kernel(
-    row_scale, column_scale, sketch_ref, tiles_ref, byrow_ref, bycol_ref, share_ref, gram_ref, *refs
+    row_scale, column_scale, sketch_ref, stored_ref, byrow_ref, bycol_ref, share_ref, gram_ref, *refs
 ):
-    send, recv = refs[:2]
-    ref = dict(zip(scratch_shapes(), refs[2:]))
+    send, recv, tiles_sem = refs[:3]
+    ref = dict(zip(scratch_shapes(), refs[3:]))
+    tiles_ref = ref["tiles"]
+    fetch = pltpu.make_async_copy(stored_ref, tiles_ref, tiles_sem)
+    fetch.start()
     row, y = lax.axis_index("rows"), lax.axis_index("cols")
     core = lax.rem(row, 2)
     x = lax.rem(lax.div(row, 2), NX)
@@ -530,6 +534,7 @@
         g0, p0, s0 = half_rows(net, 0, (sketch_ref[:, :W],), out[0])
         g1, p1, s1 = half_rows(net, 1, (sketch_ref[:, W:],), out[1])
         step(g0, g0, g1, g0, g0)
+        fetch.wait()
         p0()
         step(s0, g1, g1, s0, g1)
         p1()
@@ -607,9 +612,11 @@
             jax.ShapeDtypeStruct((4 * TILE, K), F32),
             jax.ShapeDtypeStruct((K, K), F32),
         ),
-        in_specs=[vmem, vmem, smem, smem],
+        in_specs=[vmem, pl.BlockSpec(memory_space=pl.ANY), smem, smem],
         out_specs=[vmem, vmem],
-        scratch_shapes=[pltpu.SemaphoreType.DMA((COPIES,))] * 2 + list(scratch_shapes().values()),
+        scratch_shapes=[pltpu.SemaphoreType.DMA((COPIES,))] * 2
+        + [pltpu.SemaphoreType.DMA]
+        + list(scratch_shapes().values()),
         compiler_params=pltpu.CompilerParams(
             collective_id=1, has_side_effects=True, vmem_limit_bytes=48 * MIB
         ),

time: 241 us -> 240 us (level)
  no operation moved by 1% of the time
where the time goes in v2:
time: 240 us
  Pallas kernels  237 us (99%)
    pallas_call x1, Pallas kernels, power(): pl.pallas_call(functools.partial(power_kernel, row_scale, column_scale),...  226 us
    pallas_call x1, Pallas kernels, factorize(): pl.pallas_call(functools.partial(factor_kernel, scale), name='factor_appl...  9.44 us

profile of v2, /device:TPU:1, one launch (start us, length us, event | category | flops | bytes accessed | tf_op | source)
XLA Modules:
  0.0 240.2 jit_solution(6756667280382176949)
XLA Ops:
  0.6 0.0 copy-start.1
  1.3 1.9 orders.1
  3.2 0.0 copy-start.2
  3.2 0.0 copy-start.3
  3.2 0.0 copy-done.1
  3.3 0.6 copy-done.2
  3.9 0.0 copy-done.3
  3.9 0.0 copy-start
  3.9 1.2 copy-done
  5.1 225.7 %power.1 = (f32[512,256]{1,0:T(8,128)S(1)}, f32[256,256]{1,0:T(8,128)S(1)}) custom-call(bf16[32,256]{1,0:T(8,128)(2,1)S(1)} %bitcast.7, bf16[32,128,128]{2,1,0:T(8,128)(2,1)S(1)} %bitcast.6, s32[128]{0:T(128)S(1)} %copy-done.2, s32[128]{0:T(128)S(1)} %copy-done.3), custom_call_target="tpu_custom_call" | custom-call | tf_op jit(solution)/shard_map/power/pallas_call | solution.py:608
  230.8 9.4 %factor_apply.1 = (f32[512,256]{1,0:T(8,128)}, f32[256,256]{1,0:T(8,128)}) custom-call(f32[256,256]{1,0:T(8,128)S(1)} %get-tuple-element.8.g_ref, f32[512,256]{1,0:T(8,128)S(1)} %get-tuple-element.9.y_ref), custom_call_target="tpu_custom_call" | custom-call | tf_op jit(solution)/shard_map/factor_apply/pallas_call | solution.py:176
Async XLA Ops:
  0.6 2.6 %copy-start.1 = (bf16[1,32,256]{2,1,0:T(8,128)(2,1)S(1)}, bf16[1,32,256]{2,1,0:T(8,128)(2,1)}, u32[]{:S(2)}) copy-start(bf16[1,32,256]{2,1,0:T(8,128)(2,1)} %param.9) | copy-start | bytes 49156
  3.2 0.7 copy-start.2
  3.2 0.6 copy-start.3
  3.9 1.2 copy-start

commit v3 on v2

--- a/solution.py
+++ b/solution.py
@@ -533,12 +533,12 @@
         net, out = Net(send, recv, FIRST), ([], [])
         g0, p0, s0 = half_rows(net, 0, (sketch_ref[:, :W],), out[0])
         g1, p1, s1 = half_rows(net, 1, (sketch_ref[:, W:],), out[1])
-        step(g0, g0, g1, g0, g0)
+        step(g0, g0, g1, g0, g1, g0)
         fetch.wait()
         p0()
-        step(s0, g1, g1, s0, g1)
+        step(s0, g1, g1)
         p1()
-        step(s1, s0, s1, s1)
+        step(s1, s0, s1, s0, s1)
         for h in range(2):
             for i in range(2):
                 ref["y_share"][i * 2 * TILE : (i + 1) * 2 * TILE, h * W : (h + 1) * W] = out[h][i]

time: 240 us -> 239 us (level)
  no operation moved by 1% of the time
where the time goes in v3:
time: 239 us
  Pallas kernels  236 us (99%)
    pallas_call x1, Pallas kernels, power(): pl.pallas_call(functools.partial(power_kernel, row_scale, column_scale),...  225 us
    pallas_call x1, Pallas kernels, factorize(): pl.pallas_call(functools.partial(factor_kernel, scale), name='factor_appl...  9.44 us

profile of v3, /device:TPU:1, one launch (start us, length us, event | category | flops | bytes accessed | tf_op | source)
XLA Modules:
  0.0 239.3 jit_solution(3155876045868049309)
XLA Ops:
  0.6 0.0 copy-start.1
  1.3 1.9 orders.1
  3.2 0.0 copy-start.2
  3.2 0.0 copy-start.3
  3.2 0.0 copy-done.1
  3.3 0.6 copy-done.2
  3.9 0.0 copy-done.3
  3.9 0.0 copy-start
  3.9 1.2 copy-done
  5.1 224.7 %power.1 = (f32[512,256]{1,0:T(8,128)S(1)}, f32[256,256]{1,0:T(8,128)S(1)}) custom-call(bf16[32,256]{1,0:T(8,128)(2,1)S(1)} %bitcast.7, bf16[32,128,128]{2,1,0:T(8,128)(2,1)S(1)} %bitcast.6, s32[128]{0:T(128)S(1)} %copy-done.2, s32[128]{0:T(128)S(1)} %copy-done.3), custom_call_target="tpu_custom_call" | custom-call | tf_op jit(solution)/shard_map/power/pallas_call | solution.py:608
  229.8 9.4 %factor_apply.1 = (f32[512,256]{1,0:T(8,128)}, f32[256,256]{1,0:T(8,128)}) custom-call(f32[256,256]{1,0:T(8,128)S(1)} %get-tuple-element.8.g_ref, f32[512,256]{1,0:T(8,128)S(1)} %get-tuple-element.9.y_ref), custom_call_target="tpu_custom_call" | custom-call | tf_op jit(solution)/shard_map/factor_apply/pallas_call | solution.py:176
Async XLA Ops:
  0.6 2.6 %copy-start.1 = (bf16[1,32,256]{2,1,0:T(8,128)(2,1)S(1)}, bf16[1,32,256]{2,1,0:T(8,128)(2,1)}, u32[]{:S(2)}) copy-start(bf16[1,32,256]{2,1,0:T(8,128)(2,1)} %param.9) | copy-start | bytes 49156
  3.2 0.7 copy-start.2
  3.2 0.6 copy-start.3
  3.9 1.2 copy-start
